TPU v7x, 32 devices: a whole 2x2x4 slice. The times are simulated.
32 devices in a mesh: prow: 4 (over x, core), pcol: 8 (over z, y).
Axes of the slice: x: 2, y: 2, z: 4, core: 2. Of those that a mesh axis runs over, the one named last changes fastest.
Arguments:
- matrix: bfloat16 [8, 4, 512, 4, 8, 512], P(None, 'prow', None, None, 'pcol'), may hold values from -6 to 6
- upper_inv: bfloat16 [2, 512, 512], replicated, may hold values from -4 to 4
- lower_inv: bfloat16 [2, 512, 512], replicated, may hold values from -4 to 4
- solution: bfloat16 [4, 8, 512], P(None, 'pcol'), may hold values from -0.046875 to 0.046875
- right_side: float32 [8, 4, 512], P(None, 'prow'), may hold values from -6 to 6
- diagonal_block_inverses: bfloat16 [1, 4, 512, 512], P(None, 'prow'), may hold values from -0.013671875 to 0.013671875
Outputs:
- updated: bfloat16 [8, 4, 512, 4, 8, 512], P(None, 'prow', None, None, 'pcol')
- residual: float32 [8, 4, 512], P(None, 'prow')
- precond: float32 [4, 512], replicated
All inputs are finite; a program needn't handle non-finite values.
Results may differ from a plain program's by a relative error of at most 0.0085.
Values may be sent and summed in bfloat16 or wider, within the bound.
No kernel may reach another device: no remote copies, remote signals or barrier semaphores. Data moves between devices by JAX's collectives and lax.ppermute only.
A program may use at most 128 MiB of HBM per device.

v0:
```python
import jax
import jax.numpy as jnp
from jax import lax
from jax.sharding import PartitionSpec as P

PANELS = 2


def broadcast(value, axis, source):
    kept = jnp.where(lax.axis_index(axis) == source, value, 0).astype(value.dtype)
    return lax.psum(kept, axis)


def shards(matrix, upper_inv, lower_inv, solution, right_side, diagonal_block_inverses):
    rows_blk = matrix.shape[0]
    cols_blk = matrix.shape[3]
    blk_width = matrix.shape[2]
    row_processors = lax.axis_size("prow")
    col_devs = lax.axis_size("pcol")
    col_index = lax.axis_index("pcol")
    base_matrix = matrix.reshape(rows_blk * blk_width, cols_blk * blk_width)
    current = base_matrix
    for section in range(PANELS):
        col_local = section // col_devs
        local_row_block = section // row_processors
        upper_tri = jnp.triu(upper_inv[section])
        lower_tri = jnp.tril(lower_inv[section])
        column = current[:, col_local * blk_width : (col_local + 1) * blk_width]
        row_band = current[local_row_block * blk_width : (local_row_block + 1) * blk_width, :]
        factored = jnp.dot(column, upper_tri, preferred_element_type=jnp.float32).astype(
            jnp.bfloat16
        )
        left_panel = broadcast(factored, "pcol", section % col_devs)
        top_local = jnp.dot(lower_tri, row_band, preferred_element_type=jnp.float32).astype(
            jnp.bfloat16
        )
        top_panel = broadcast(top_local, "prow", section % row_processors)
        current = (
            current.astype(jnp.float32)
            - jnp.dot(left_panel, top_panel, preferred_element_type=jnp.float32)
        ).astype(jnp.bfloat16)
    partial_value = jnp.dot(
        base_matrix, solution.reshape(cols_blk * blk_width), preferred_element_type=jnp.float32
    )
    totals = lax.psum(partial_value, "pcol")
    residual = right_side.reshape(rows_blk * blk_width) - totals
    res_blocks = residual.reshape(rows_blk, blk_width)
    slot_count = diagonal_block_inverses.shape[0]
    inverses = diagonal_block_inverses.reshape(slot_count, blk_width, blk_width)
    solve_count = slot_count * row_processors
    col_blocks = base_matrix.reshape(rows_blk * blk_width, cols_blk, blk_width)

    def carry_forward(blk_id, state):
        accum, solved = state
        owner_row = blk_id % row_processors
        slot_id = blk_id // row_processors
        pending = lax.dynamic_slice_in_dim(accum, slot_id * blk_width, blk_width, 0)
        res_block = lax.dynamic_slice_in_dim(res_blocks, slot_id, 1, 0)[0]
        inv_block = inverses[0].astype(jnp.float32)
        row_total = lax.psum(pending, "pcol")
        local_value = jnp.dot(inv_block, res_block - row_total, precision=lax.Precision.HIGHEST)
        new_value = broadcast(local_value, "prow", owner_row)
        rounded = new_value.astype(jnp.bfloat16)
        has_col = col_index == blk_id % col_devs
        col_piece = lax.dynamic_slice_in_dim(col_blocks, blk_id // col_devs, 1, 1)[:, 0, :]
        product = jnp.dot(col_piece, rounded, preferred_element_type=jnp.float32)
        accum = accum + jnp.where(has_col, product, jnp.zeros_like(product))
        solved = lax.dynamic_update_slice_in_dim(solved, new_value[None], blk_id, 0)
        return (accum, solved)

    start = (
        jnp.zeros((rows_blk * blk_width,), jnp.float32),
        jnp.zeros((solve_count, blk_width), jnp.float32),
    )
    precond = lax.fori_loop(0, solve_count, carry_forward, start)[1]
    return (current.reshape(matrix.shape), residual.reshape(right_side.shape), precond)


def solution(mesh):
    return jax.shard_map(
        shards,
        mesh=mesh,
        in_specs=(
            P(None, "prow", None, None, "pcol", None),
            P(),
            P(),
            P(None, "pcol", None),
            P(None, "prow", None),
            P(None, "prow", None, None),
        ),
        out_specs=(P(None, "prow", None, None, "pcol", None), P(None, "prow", None), P()),
        check_vma=False,
    )
```

profile of v0, /device:TPU:0, one launch (start us, length us, event | category | flops | bytes accessed | tf_op | source)
XLA Modules:
  0.0 525.7 jit_solution(17538613553749353497)
XLA Ops:
  7.2 0.0 all-reduce.7.cloned.1.call-start
  7.2 1.5 slice-done
  8.8 1.9 copy.13
  10.7 4.2 fusion.11
  14.9 0.0 all-reduce.5.cloned.1.call-start
  15.0 11.6 %copy.12 = bf16[512,8,4,512]{3,1,2,0:T(8,128)(2,1)S(1)} copy(bf16[512,8,4,512]{3,2,1,0:T(4,128)(2,1)} %bitcast.75) | data formatting | bytes 33554432
  26.6 6.1 %copy-done = bf16[512,8,4,512]{3,1,2,0:T(8,128)(2,1)} copy-done((bf16[512,8,4,512]{3,1,2,0:T(8,128)(2,1)}, bf16[512,8,4,512]{3,1,2,0:T(8,128)(2,1)S(1)}, u32[]{:S(2)}) %copy-start) | copy-done | bytes 16777240
  32.8 4.6 fusion.7
  37.3 0.0 all-reduce.11.cloned.1.call-start
  37.4 0.6 copy-done.4
  38.0 31.1 %all-reduce.7.cloned.1.call-done = bf16[512,2048]{1,0:T(8,128)(2,1)} async-done(((bf16[512,2048]{1,0:T(8,128)(2,1)}), bf16[512,2048]{1,0:T(8,128)(2,1)}) %all-reduce.7.cloned.1.call-update) | async-done | bytes 2097168 | tf_op jit(solution)/shard_map/psum | solution.py:11
  69.1 160.5 %all-reduce.5.cloned.1.call-done = bf16[4096,512]{0,1:T(8,128)(2,1)} async-done(((bf16[4096,512]{0,1:T(8,128)(2,1)}), bf16[4096,512]{0,1:T(8,128)(2,1)}) %all-reduce.5.cloned.1.call-update) | async-done | bytes 4194320 | tf_op jit(solution)/shard_map/psum | solution.py:11
  229.7 17.4 %subtract_convert_fusion.1 = bf16[4096,2048]{1,0:T(8,128)(2,1)} fusion(bf16[4096,2048]{1,0:T(8,128)(2,1)} %bitcast.78, bf16[4096,512]{0,1:T(8,128)(2,1)} %all-reduce.5.cloned.1.call-done, bf16[512,2048]{1,0:T(8,128)(2,1)} %all-reduce.7.cloned.1.call-done), kind=kOutput, calls=%fused_computation.11 | convolution fusion | flops 8615100416 | bytes 39845888 | tf_op jit(solution)/shard_map/dot_general | solution.py:40
  247.1 4.2 fusion.12
  251.3 0.2 all-reduce.9.cloned.1.call-start
  251.5 10.6 %fusion.40 = f32[1,4096]{1,0:T(1,128)S(1)} fusion(bf16[4096,2048]{1,0:T(8,128)(2,1)} %bitcast.79, bf16[2048,1]{0,1:T(2,128)(2,1)S(1)} %bitcast.90), kind=kOutput, calls=%fused_computation.50 | convolution fusion | flops 16777216 | bytes 16797696 | tf_op jit(solution)/shard_map/dot_general | solution.py:42
  262.1 16.3 %copy.10 = bf16[8,1,512,4,1,512]{5,2,0,3,4,1:T(8,128)(2,1)} copy(bf16[8,1,512,4,1,512]{5,3,4,2,1,0:T(4,128)(2,1)} %param.8) | data formatting | bytes 33554432 | tf_op args[0]
  278.4 34.4 %psum.69 = f32[4096]{0:T(1024)S(1)} all-reduce(f32[4096]{0:T(1024)S(1)} %bitcast.88), channel_id=1, replica_groups=mesh['prow'=4,'pcol'=8] {'pcol'}, use_global_device_ids=true, to_apply=%region_4.5 | all-reduce | flops 4096 | bytes 32768 | tf_op jit(solution)/shard_map/psum | solution.py:45
  312.9 6.6 %fusion.8 = bf16[4096,512]{1,0:T(8,128)(2,1)} fusion(bf16[4096,2048]{1,0:T(8,128)(2,1)} %subtract_convert_fusion.1, pred[]{:T(512)S(6)} %eq.51, bf16[2,512,512]{2,1,0:T(8,128)(2,1)S(1)} %copy-done.6, s32[512]{0:T(512)S(1)} %iota_add_fusion), kind=kOutput, calls=%fused_computation.16 | convolution fusion | flops 2152202240 | bytes 8914945 | tf_op jit(solution)/shard_map/dot_general | solution.py:30
  319.5 1.0 copy-done.1
  320.5 119.5 %while.19 = (s32[]{:T(128)}, f32[4096]{0:T(1024)S(1)}, f32[4,512]{1,0:T(4,128)}, s32[]{:T(128)}, bf16[4096,4,512]{2,0,1:T(8,128)(2,1)}, /*index=5*/f32[8,512]{1,...) while((s32[]{:T(128)}, f32[4096]{0:T(1024)S(1)}, ...), condition=%wide.region_8.9_spmd.clone, body=%wide.region_5.8_spmd.clone.sunk | while | flops 7359016 | bytes 4858435 | solution.py:75
  320.5 0.1 dynamic_slice.46
  320.6 17.9 %psum.74 = f32[512]{0:T(512)S(1)} all-reduce(f32[512]{0:T(512)S(1)} %dynamic_slice.46), channel_id=1, replica_groups=mesh['prow'=4,'pcol'=8] {'pcol'}, use_global_device_ids=true, to_apply=%region_6.6 | all-reduce | flops 512 | bytes 4096 | tf_op jit(solution)/shard_map/while/body/eval_jaxpr/psum | solution.py:60
  338.4 0.5 fusion.60
  339.0 6.1 %psum.75 = f32[512]{0:T(512)S(1)} all-reduce(f32[512]{0:T(512)S(1)} %broadcast_select_fusion.5), channel_id=1, replica_groups=mesh['prow'=4,'pcol'=8] {'prow'}, use_global_device_ids=true, to_apply=%region_7.7 | all-reduce | flops 512 | bytes 4096 | tf_op jit(solution)/shard_map/while/body/eval_jaxpr/psum | solution.py:11
  345.0 1.3 dynamic_update_slice.13
  346.3 3.4 fusion.61
  349.8 0.1 dynamic_slice.46
  349.8 20.2 %psum.74 = f32[512]{0:T(512)S(1)} all-reduce(f32[512]{0:T(512)S(1)} %dynamic_slice.46), channel_id=1, replica_groups=mesh['prow'=4,'pcol'=8] {'pcol'}, use_global_device_ids=true, to_apply=%region_6.6 | all-reduce | flops 512 | bytes 4096 | tf_op jit(solution)/shard_map/while/body/eval_jaxpr/psum | solution.py:60
  370.0 0.5 fusion.60
  370.5 5.7 %psum.75 = f32[512]{0:T(512)S(1)} all-reduce(f32[512]{0:T(512)S(1)} %broadcast_select_fusion.5), channel_id=1, replica_groups=mesh['prow'=4,'pcol'=8] {'prow'}, use_global_device_ids=true, to_apply=%region_7.7 | all-reduce | flops 512 | bytes 4096 | tf_op jit(solution)/shard_map/while/body/eval_jaxpr/psum | solution.py:11
  376.2 1.3 dynamic_update_slice.13
  377.5 3.4 fusion.61
  380.9 0.1 dynamic_slice.46
  381.0 17.6 %psum.74 = f32[512]{0:T(512)S(1)} all-reduce(f32[512]{0:T(512)S(1)} %dynamic_slice.46), channel_id=1, replica_groups=mesh['prow'=4,'pcol'=8] {'pcol'}, use_global_device_ids=true, to_apply=%region_6.6 | all-reduce | flops 512 | bytes 4096 | tf_op jit(solution)/shard_map/while/body/eval_jaxpr/psum | solution.py:60
  398.7 0.5 fusion.60
  399.2 5.7 %psum.75 = f32[512]{0:T(512)S(1)} all-reduce(f32[512]{0:T(512)S(1)} %broadcast_select_fusion.5), channel_id=1, replica_groups=mesh['prow'=4,'pcol'=8] {'prow'}, use_global_device_ids=true, to_apply=%region_7.7 | all-reduce | flops 512 | bytes 4096 | tf_op jit(solution)/shard_map/while/body/eval_jaxpr/psum | solution.py:11
  404.9 1.3 dynamic_update_slice.13
  406.2 3.4 fusion.61
  409.6 0.1 dynamic_slice.46
  409.7 19.1 %psum.74 = f32[512]{0:T(512)S(1)} all-reduce(f32[512]{0:T(512)S(1)} %dynamic_slice.46), channel_id=1, replica_groups=mesh['prow'=4,'pcol'=8] {'pcol'}, use_global_device_ids=true, to_apply=%region_6.6 | all-reduce | flops 512 | bytes 4096 | tf_op jit(solution)/shard_map/while/body/eval_jaxpr/psum | solution.py:60
  428.7 0.5 fusion.60
  429.2 6.1 %psum.75 = f32[512]{0:T(512)S(1)} all-reduce(f32[512]{0:T(512)S(1)} %broadcast_select_fusion.5), channel_id=1, replica_groups=mesh['prow'=4,'pcol'=8] {'prow'}, use_global_device_ids=true, to_apply=%region_7.7 | all-reduce | flops 512 | bytes 4096 | tf_op jit(solution)/shard_map/while/body/eval_jaxpr/psum | solution.py:11
  435.3 1.3 dynamic_update_slice.13
  436.6 3.4 fusion.61
  440.1 34.0 %all-reduce.9.cloned.1.call-done = bf16[4096,512]{1,0:T(8,128)(2,1)} async-done(((bf16[4096,512]{1,0:T(8,128)(2,1)}), bf16[4096,512]{1,0:T(8,128)(2,1)}) %all-reduce.9.cloned.1.call-update) | async-done | bytes 4194320 | tf_op jit(solution)/shard_map/psum | solution.py:11
  474.1 17.3 %subtract_convert_fusion = bf16[4096,2048]{1,0:T(8,128)(2,1)} fusion(bf16[4096,2048]{1,0:T(8,128)(2,1)} %subtract_convert_fusion.1, bf16[4096,512]{1,0:T(8,128)(2,1)} %all-reduce.9.cloned.1.call-done, bf16[512,2048]{1,0:T(8,128)(2,1)} %all-reduce.11.cloned.1.call-done), kind=kOutput, calls=%fused_computation.10 | convolution fusion | flops 8615100416 | bytes 39845888 | tf_op jit(solution)/shard_map/dot_general | solution.py:40
  491.4 27.8 %reshape.40 = bf16[8,1,512,4,1,512]{5,3,2,0,4,1:T(4,128)(2,1)} reshape(bf16[4096,2048]{1,0:T(8,128)(2,1)} %subtract_convert_fusion) | data formatting | bytes 33554432 | tf_op jit(solution)/shard_map/reshape | solution.py:76
  (51 shorter events, 0.3 us)
Async XLA Ops:
  7.2 1.6 slice-start
  7.2 62.0 %all-reduce.7.cloned.1.call-start = ((), (), s32[]{:S(2)}) async-start(), calls=%async_computation.1 | async-start | bytes 4194304 | tf_op jit(solution)/shard_map/psum | solution.py:11
  7.2 3.5 copy-start.5
  14.9 214.8 %all-reduce.5.cloned.1.call-start = ((), (), s32[]{:S(2)}) async-start(), calls=%async_computation | async-start | bytes 8388608 | tf_op jit(solution)/shard_map/psum | solution.py:11
  15.0 17.8 %copy-start.6 = (bf16[2,512,512]{2,1,0:T(8,128)(2,1)S(1)}, bf16[2,512,512]{2,1,0:T(8,128)(2,1)}, u32[]{:S(2)}) copy-start(bf16[2,512,512]{2,1,0:T(8,128)(2,1)} %param.9) | copy-start | bytes 3145732
  26.6 6.2 %copy-start = (bf16[512,8,4,512]{3,1,2,0:T(8,128)(2,1)}, bf16[512,8,4,512]{3,1,2,0:T(8,128)(2,1)S(1)}, u32[]{:S(2)}) copy-start(bf16[512,8,4,512]{3,1,2,0:T(8,128)(2,1)S(1)} %copy.12) | copy-start | bytes 50331652
  37.3 0.7 copy-start.4
  37.3 402.7 %all-reduce.11.cloned.1.call-start = ((), (), s32[]{:S(2)}) async-start(), calls=%async_computation.3 | async-start | bytes 4194304 | tf_op jit(solution)/shard_map/psum | solution.py:11
  251.3 222.8 %all-reduce.9.cloned.1.call-start = ((), (), s32[]{:S(2)}) async-start(), calls=%async_computation.2 | async-start | bytes 8388608 | tf_op jit(solution)/shard_map/psum | solution.py:11
  262.1 50.7 %copy-start.3 = (f32[8,1,512]{2,1,0:T(1,128)S(1)}, f32[8,1,512]{2,1,0:T(1,128)}, u32[]{:S(2)}) copy-start(f32[8,1,512]{2,1,0:T(1,128)} %param.12) | copy-start | bytes 49156
  312.9 6.6 %copy-start.2 = (f32[4096]{0:T(1024)}, f32[4096]{0:T(1024)S(1)}, u32[]{:S(2)}) copy-start(f32[4096]{0:T(1024)S(1)} %sub.33) | copy-start | bytes 49156
  319.5 1.0 copy-start.1
Sparse Core Ops, SparseCore 0:
  15.0 54.0 all-reduce.6
  73.3 156.3 all-reduce.4
  251.4 50.3 all-reduce.10
  319.6 154.4 all-reduce.8
where the time goes:
time: 527 us; the launch traced here: 526 us
  waiting for transfers between devices  226 us (43%)
  blocking collectives  133 us (25%)
  matrix products  80.3 us (15%)
  local copies, waits for them, and re-layouts  72.6 us (14%)
  between operations  13.9 us (3%)
    psum x4, waiting for transfers between devices, broadcast(): return lax.psum(kept, axis)  226 us
    psum x4, blocking collectives, carry_forward(): row_total = lax.psum(pending, 'pcol')  74.7 us
    unnamed x18, local copies, waits for them, and re-layouts  37.7 us
    dot_general x2, matrix products, shards(): jnp.dot(left_panel, top_panel, preferred_element_type=jnp.float32)  34.7 us
    psum x1, blocking collectives, shards(): totals = lax.psum(partial_value, 'pcol')  34.4 us
    reshape x1, local copies, waits for them, and re-layouts, shards(): current.reshape(matrix.shape)  27.8 us
    psum x4, blocking collectives, broadcast(): return lax.psum(kept, axis)  23.4 us
    dot_general x4, matrix products, carry_forward(): product = jnp.dot(col_piece, rounded, preferred_element_type=jnp.float32)  13.5 us
  transfers between devices with their start and end apart: 4, of which 3 were waited for; matrix products, arithmetic and copies ran while one was open for 13% of the time, Pallas kernels for 0%

commit v1 on v0

v1 whole, which is shorter than its diff:
```python
import jax
import jax.numpy as jnp
from jax import lax
from jax.experimental import pallas as pl
from jax.experimental.pallas import tpu as pltpu
from jax.sharding import PartitionSpec as P

LANES = 128
VMEM_BYTES = 48 * 1024 * 1024
F32 = jnp.float32
BF16 = jnp.bfloat16


def matmul(a, b):
    return jnp.dot(a, b, preferred_element_type=F32)


def extract_kernel(groups, stride, a_ref, sol_ref, col_ref, part_ref, wide):
    rows = col_ref.shape[0]
    wide[...] = a_ref[...].astype(F32)
    total = jnp.zeros((rows, LANES), F32)
    for g in range(groups):
        piece = wide[pl.ds(g, rows, stride=groups), :]
        if g % stride == 0:
            col_ref[:, pl.ds(g // stride * LANES, LANES)] = piece.astype(BF16)
        total = total + piece * sol_ref[g : g + 1, :].astype(F32)
    ones = jnp.ones((8, LANES), F32)
    sums = lax.dot_general(
        ones, total, (((1,), (1,)), ((), ())), precision=lax.Precision.HIGHEST, preferred_element_type=F32
    )
    part_ref[...] = sums[0:1, :]


def extract(flat, sol, first, rows, groups, stride, width):
    size = rows * groups
    assert (first * groups) % size == 0
    at = first * groups // size
    return pl.pallas_call(
        lambda *refs: extract_kernel(groups, stride, *refs),
        grid=(1,),
        in_specs=[
            pl.BlockSpec((size, LANES), lambda i: (at, 0)),
            pl.BlockSpec((groups, LANES), lambda i: (0, 0)),
        ],
        out_specs=[
            pl.BlockSpec((rows, width), lambda i: (0, 0)),
            pl.BlockSpec((1, rows), lambda i: (0, 0)),
        ],
        out_shape=[
            jax.ShapeDtypeStruct((rows, width), BF16),
            jax.ShapeDtypeStruct((1, rows), F32),
        ],
        scratch_shapes=[pltpu.VMEM((size, LANES), F32)],
        compiler_params=pltpu.CompilerParams(vmem_limit_bytes=VMEM_BYTES),
        cost_estimate=pl.CostEstimate(flops=4 * size * LANES, bytes_accessed=size * LANES * 2, transcendentals=0),
        name="extract",
    )(flat, sol)


def factor_kernel(groups, where_ref, mine_ref, other_ref, blk_mine_ref, blk_other_ref, up_ref, low_ref, v_ref, bands, blocks):
    core = where_ref[0]
    lane = where_ref[1]
    width = up_ref.shape[1]
    bands[core] = mine_ref[...].astype(F32)
    bands[1 - core] = other_ref[...].astype(F32)
    blocks[core] = blk_mine_ref[...]
    blocks[1 - core] = blk_other_ref[...]
    row = lax.broadcasted_iota(jnp.int32, (width, width), 0)
    col = lax.broadcasted_iota(jnp.int32, (width, width), 1)
    zero = jnp.zeros((width, width), BF16)
    upper = [jnp.where(row <= col, up_ref[s], zero) for s in range(2)]
    lower = [jnp.where(row >= col, low_ref[s], zero) for s in range(2)]
    top_01 = matmul(lower[0], blocks[0]).astype(BF16)
    left_10 = matmul(blocks[1], upper[0]).astype(BF16)

    def step(n, carry):
        def band(s):
            return jnp.concatenate(
                [bands[s, pl.ds(2 * n + h, width, stride=groups), :] for h in range(2)], axis=1
            )

        top_0 = matmul(lower[0], band(0).astype(BF16)).astype(BF16)
        rest = (band(1) - matmul(left_10, top_0)).astype(BF16)
        top_1 = matmul(lower[1], rest).astype(BF16)
        v_1 = matmul(upper[1], top_1).astype(BF16)
        mixed = (top_0.astype(F32) - matmul(top_01, v_1)).astype(BF16)
        v_0 = matmul(upper[0], mixed).astype(BF16)
        at = pl.ds(pl.multiple_of(n * 2 * LANES, 2 * LANES), 2 * LANES)
        v_ref[lane, :, at] = v_0
        v_ref[1 - lane, :, at] = v_1
        return carry

    lax.fori_loop(0, groups // 2, step, 0)


def factors(where, mine, other, blk_mine, blk_other, upper, lower, groups):
    width = upper.shape[1]
    cols = groups * LANES
    vmem = pl.BlockSpec(memory_space=pltpu.VMEM)
    return pl.pallas_call(
        lambda *refs: factor_kernel(groups, *refs),
        in_specs=[pl.BlockSpec(memory_space=pltpu.SMEM)] + [vmem] * 6,
        out_specs=vmem,
        out_shape=jax.ShapeDtypeStruct((2, width, cols), BF16),
        scratch_shapes=[
            pltpu.VMEM((2, width * groups, LANES), F32),
            pltpu.VMEM((2, width, width), BF16),
        ],
        compiler_params=pltpu.CompilerParams(vmem_limit_bytes=VMEM_BYTES),
        cost_estimate=pl.CostEstimate(flops=12 * width * width * cols, bytes_accessed=12 * width * cols, transcendentals=0),
        name="factors",
    )(where, mine, other, blk_mine, blk_other, upper, lower)


def update_kernel(groups, a_ref, mine_ref, other_ref, v_ref, *rest):
    out_ref, wide = rest[-2:]
    rows = mine_ref.shape[0]
    for n in range(groups // 2):
        at = slice(n * 2 * LANES, (n + 1) * 2 * LANES)
        value = matmul(mine_ref[...], v_ref[0, :, at]) + matmul(other_ref[...], v_ref[1, :, at])
        for h in range(2):
            wide[pl.ds(2 * n + h, rows, stride=groups), :] = value[:, h * LANES : (h + 1) * LANES]
    out_ref[...] = (a_ref[...].astype(F32) - wide[...]).astype(BF16)


def update(flat, mine, other, v, out, first, groups):
    rows, width = mine.shape
    sub = min(rows, 256)
    size = sub * groups
    base = first // sub
    cols = groups * LANES
    in_specs = [
        pl.BlockSpec((size, LANES), lambda i: (base + i, 0)),
        pl.BlockSpec((sub, width), lambda i: (i, 0)),
        pl.BlockSpec((sub, width), lambda i: (i, 0)),
        pl.BlockSpec((2, width, cols), lambda i: (0, 0, 0)),
    ]
    args = [flat, mine, other, v]
    aliases = {}
    if out is not None:
        in_specs.append(pl.BlockSpec(memory_space=pl.ANY))
        args.append(out)
        aliases = {4: 0}
    return pl.pallas_call(
        lambda *refs: update_kernel(groups, *refs),
        grid=(rows // sub,),
        in_specs=in_specs,
        out_specs=pl.BlockSpec((size, LANES), lambda i: (base + i, 0)),
        out_shape=jax.ShapeDtypeStruct(flat.shape, BF16),
        scratch_shapes=[pltpu.VMEM((size, LANES), F32)],
        input_output_aliases=aliases,
        compiler_params=pltpu.CompilerParams(vmem_limit_bytes=VMEM_BYTES),
        cost_estimate=pl.CostEstimate(
            flops=4 * rows * width * cols, bytes_accessed=4 * rows * cols + 4 * rows * width + 4 * width * cols, transcendentals=0
        ),
        name="update",
    )(*args)


def solve_kernel(place_ref, state_ref, res_ref, inv_ref, *rest):
    cols, out_ref = rest[:-1], rest[-1]
    place = place_ref[0]
    width = inv_ref.shape[0]
    nt = (((1,), (1,)), ((), ()))
    pending = jnp.zeros((8, width), F32)
    for j, col in enumerate(cols):
        known = jnp.where(j < place, state_ref[j : j + 1, :], 0.0)
        pending = pending + lax.dot_general(
            jnp.broadcast_to(known, (8, width)).astype(BF16), col[...], nt, preferred_element_type=F32
        )
    left = res_ref[...] - pending[0:1, :]
    high = left.astype(BF16)
    rest_1 = left - high.astype(F32)
    mid = rest_1.astype(BF16)
    low = (rest_1 - mid.astype(F32)).astype(BF16)
    total = jnp.zeros((8, width), F32)
    for piece in (low, mid, high):
        wide = jnp.broadcast_to(piece.astype(F32), (8, width)).astype(BF16)
        total = total + lax.dot_general(wide, inv_ref[...], nt, preferred_element_type=F32)
    row = lax.broadcasted_iota(jnp.int32, state_ref.shape, 0)
    out_ref[...] = jnp.where(row == place, jnp.broadcast_to(total[0:1, :], state_ref.shape), state_ref[...])


def solve_step(place, state, res, inv, cols):
    vmem = pl.BlockSpec(memory_space=pltpu.VMEM)
    return pl.pallas_call(
        solve_kernel,
        in_specs=[pl.BlockSpec(memory_space=pltpu.SMEM)] + [vmem] * (3 + len(cols)),
        out_specs=vmem,
        out_shape=jax.ShapeDtypeStruct(state.shape, F32),
        compiler_params=pltpu.CompilerParams(vmem_limit_bytes=VMEM_BYTES),
        cost_estimate=pl.CostEstimate(
            flops=2 * inv.size * (len(cols) + 3), bytes_accessed=2 * inv.size * (len(cols) + 1), transcendentals=0
        ),
        name="solve",
    )(place, state, res, inv, *cols)


def after(value, *others):
    return lax.optimization_barrier((value, *others))[0]


def shards(matrix, upper_inv, lower_inv, solution, right_side, diagonal_block_inverses):
    slots, _, width, col_slots, _, _ = matrix.shape
    n_prow = lax.axis_size("prow")
    n_pcol = lax.axis_size("pcol")
    ny = n_prow // 2
    nz = n_pcol // ny
    prow = lax.axis_index("prow")
    pcol = lax.axis_index("pcol")
    z, y = pcol // ny, pcol % ny
    core, lane = prow % 2, y % 2
    lane_tiles = width // LANES
    groups = lane_tiles * col_slots
    rows = slots * width
    flat = matrix.reshape(rows, col_slots, lane_tiles, LANES).transpose(0, 2, 1, 3).reshape(rows * groups, LANES)
    sol = solution.reshape(col_slots, lane_tiles, LANES).transpose(1, 0, 2).reshape(groups, LANES)

    def spread(value, axis, size):
        for s in range(2, size, 2):
            got = lax.ppermute(value, axis, [(s - 2, s), (s - 1, s + 1)])
            value = jnp.where(lax.axis_index(axis) // 2 == s // 2, got, value)
        return value

    def swap(value, axis, size, bit=1):
        return lax.ppermute(value, axis, [(i, i ^ bit) for i in range(size)])

    band = flat[: width * groups]
    band_mine = spread(band, "prow", n_prow)
    band_other = swap(band_mine, "prow", n_prow)

    def along_z(pairs):
        return [(a * ny + k, b * ny + k) for a, b in pairs for k in range(2)]

    def send_down(local):
        value = local
        step = nz // 2
        held = [0]
        while step:
            if held == [0]:
                moves = [[(0, step)]]
            else:
                moves = [[(m, m - step) for m in held], [(m, m + step) for m in held]]
            got = [(lax.ppermute(value, "pcol", along_z(m)), m) for m in moves]
            for arrived, m in got:
                mask = z == m[0][1]
                for _, b in m[1:]:
                    mask = mask | (z == b)
                value = jnp.where(mask, arrived, value)
            held = [b for m in moves for _, b in m]
            step //= 2
        for s in range(2, ny, 2):
            pairs = [(a * ny + s - 2 + k, a * ny + s + k) for a in range(nz) for k in range(2)]
            got_y = lax.ppermute(value, "pcol", pairs)
            value = jnp.where(y // 2 == s // 2, got_y, value)
        other = swap(value, "pcol", n_pcol)
        return value, other

    column, parts = [], []
    for c in range(slots):
        col, part = extract(flat, sol, c * width, width, groups, col_slots, width)
        column.append(col)
        parts.append(part)
    mine, other = [], []
    for c in range(slots):
        local = column[c]
        if c >= 2:
            local = after(local, mine[c - 2])
        m, o = send_down(local)
        mine.append(m)
        other.append(o)

    pick = jnp.where(core != lane, mine[0], other[0])
    blk_mine = spread(pick, "prow", n_prow)
    blk_other = swap(blk_mine, "prow", n_prow)

    total = jnp.concatenate(parts, axis=0)
    bit = 1
    while bit < n_pcol:
        total = total + swap(total, "pcol", n_pcol, bit)
        bit *= 2
    residual = right_side.reshape(slots, width) - total

    count = n_prow * diagonal_block_inverses.shape[0]
    assert diagonal_block_inverses.shape[0] == 1
    home = count - 2
    inv = diagonal_block_inverses.reshape(width, width)
    needed = [jnp.where(lane == 0, mine[0], other[0]), jnp.where(lane == 0, other[0], mine[0])]
    for j in range(2, home):
        needed.append(lax.ppermute(column[0], "pcol", [(j, home)]))
    needed.append(column[0])
    place = prow.astype(jnp.int32).reshape(1)
    state = jnp.zeros((count, width), F32)
    for k in range(count):
        if k:
            state = lax.ppermute(state, "prow", [(i, i + 1) for i in range(n_prow - 1)])
        state = solve_step(place, state, residual[0:1], inv, needed)
    state = jnp.where((prow == n_prow - 1) & (pcol == home), state, 0.0)
    for axis, size in (("prow", n_prow), ("pcol", n_pcol)):
        bit = 1
        while bit < size:
            state = state + swap(state, axis, size, bit)
            bit *= 2

    where = jnp.stack([core, lane]).astype(jnp.int32)
    v = factors(where, band_mine, band_other, blk_mine, blk_other, upper_inv, lower_inv, groups)
    out = None
    for c in range(slots):
        out = update(flat, mine[c], other[c], v, out, c * width, groups)
    updated = out.reshape(rows, lane_tiles, col_slots, LANES).transpose(0, 2, 1, 3).reshape(matrix.shape)
    return (updated, residual.reshape(right_side.shape), state)


def solution(mesh):
    return jax.shard_map(
        shards,
        mesh=mesh,
        in_specs=(
            P(None, "prow", None, None, "pcol", None),
            P(),
            P(),
            P(None, "pcol", None),
            P(None, "prow", None),
            P(None, "prow", None, None),
        ),
        out_specs=(P(None, "prow", None, None, "pcol", None), P(None, "prow", None), P()),
        check_vma=False,
    )
```

time: 527 us -> 317 us (0.60)
  waiting for transfers between devices: 226 us -> 63.2 us
  blocking collectives: 133 us -> 0 us
  starting transfers between devices: 0.34 us -> 121 us
  Pallas kernels: 0 us -> 99.4 us
  matrix products: 80.3 us -> 0 us
  local copies, waits for them, and re-layouts: 72.6 us -> 11.9 us
  other arithmetic: 0.14 us -> 15.3 us
  between operations: 13.9 us -> 1.44 us
    psum x4 -> x0, waiting for transfers between devices: 226 us -> none  [broadcast(): return lax.psum(kept, axis)]
    psum x9 -> x0, blocking collectives: 133 us -> none  [the longest x4 74.7 us: carry_forward(): row_total = lax.psum(pending, 'pcol')]
    ppermute x0 -> x47, starting transfers between devices: none -> 121 us  [the longest x24 67.2 us: send_down(): got = [(lax.ppermute(value, 'pcol', along_z(m)), m) for m in moves]]
    pallas_call x0 -> x21, Pallas kernels: none -> 99.4 us  [the longest x8 46.4 us: update(): pl.pallas_call(lambda *refs: update_kernel(groups, *refs), grid=(rows //...]
    dot_general x15 -> x0, matrix products: 80.3 us -> none  [the longest x2 34.7 us: shards(): jnp.dot(left_panel, top_panel, preferred_element_type=jnp.float32)]
    ppermute x0 -> x47, waiting for transfers between devices: none -> 63.2 us  [the longest x24 31.2 us: send_down(): got = [(lax.ppermute(value, 'pcol', along_z(m)), m) for m in moves]]
    unnamed x18 -> x35, local copies, waits for them, and re-layouts: 37.7 us -> 8.24 us
    reshape x2 -> x0, local copies, waits for them, and re-layouts: 27.8 us -> none  [the longest x1 27.8 us: shards(): current.reshape(matrix.shape)]
  transfers between devices with their start and end apart: 4 -> 47, of which waited for: 3 -> 16; matrix products, arithmetic and copies ran while one was open for 13% -> 6% of each run, Pallas kernels for 0% -> 29%
where the time goes in v1:
time: 317 us; the launch traced here: 312 us
  starting transfers between devices  121 us (38%)
  Pallas kernels  99.4 us (31%)
  waiting for transfers between devices  63.2 us (20%)
  other arithmetic  15.3 us (5%)
  local copies, waits for them, and re-layouts  11.9 us (4%)
    ppermute x24, starting transfers between devices, send_down(): got = [(lax.ppermute(value, 'pcol', along_z(m)), m) for m in moves]  67.2 us
    pallas_call x8, Pallas kernels, update(): pl.pallas_call(lambda *refs: update_kernel(groups, *refs), grid=(rows //...  46.4 us
    ppermute x24, waiting for transfers between devices, send_down(): got = [(lax.ppermute(value, 'pcol', along_z(m)), m) for m in moves]  31.2 us
    ppermute x18, waiting for transfers between devices, swap(): return lax.ppermute(value, axis, [(i, i ^ bit) for i in range(size)])  30.1 us
    ppermute x3, starting transfers between devices, shards(): state = lax.ppermute(state, 'prow', [(i, i + 1) for i in range(n_prow - 1)])  29 us
    pallas_call x8, Pallas kernels, extract(): pl.pallas_call(lambda *refs: extract_kernel(groups, stride, *refs), grid=...  26.7 us
    pallas_call x1, Pallas kernels, factors(): pl.pallas_call(lambda *refs: factor_kernel(groups, *refs), in_specs=[pl.B...  22.4 us
    ppermute x18, starting transfers between devices, swap(): return lax.ppermute(value, axis, [(i, i ^ bit) for i in range(size)])  17.6 us
  transfers between devices with their start and end apart: 47, of which 16 were waited for; matrix products, arithmetic and copies ran while one was open for 6% of the time, Pallas kernels for 29%

profile of v1, /device:TPU:0, one launch (start us, length us, event | category | flops | bytes accessed | tf_op | source)
XLA Modules:
  0.0 312.3 jit_solution(3944852897444740680)
XLA Ops:
  1.3 3.3 %extract.12 = (bf16[512,512]{1,0:T(8,128)(2,1)S(1)}, f32[1,512]{1,0:T(1,128)S(1)}) custom-call(bf16[65536,128]{1,0:T(8,128)(2,1)} %bitcast.35, bf16[16,128]{1,0:T(8,128)(2,1)S(1)} %bitcast.27), custom_call_target="tpu_custom_call" | custom-call | flops 4194304 | bytes 2097152 | tf_op jit(solution)/shard_map/extract/pallas_call | solution.py:38
  4.6 6.0 %collective-permute-start.15 = (bf16[512,512]{1,0:T(8,128)(2,1)S(1)}, bf16[512,512]{1,0:T(8,128)(2,1)S(1)}, u32[]{:S(2)}, u32[]{:S(2)}) collective-permute-start(bf16[512,512]{1,0:T(8,128)(2,1)S(1)} %get-tuple-element.32.rest_2_), channel_id=1, source_target_pairs={{0,4},{1,5},{8,12},{9,13},{16,20},{17,21},{24,28},{25,29}} | collective-permute-start | bytes 1572872 | tf_op jit(solution)/shard_map/ppermute | solution.py:244
  10.6 11.1 %collective-permute-done.15 = bf16[512,512]{1,0:T(8,128)(2,1)S(1)} collective-permute-done((bf16[512,512]{1,0:T(8,128)(2,1)S(1)}, bf16[512,512]{1,0:T(8,128)(2,1)S(1)}, u32[]{:S(2)}, u32[]{:S(2)}) %collective-permute-start.15) | collective-permute-done | bytes 524320 | tf_op jit(solution)/shard_map/ppermute | solution.py:244
  24.0 3.3 %extract.11 = (bf16[512,512]{1,0:T(8,128)(2,1)S(1)}, f32[1,512]{1,0:T(1,128)S(1)}) custom-call(bf16[65536,128]{1,0:T(8,128)(2,1)} %bitcast.36, bf16[16,128]{1,0:T(8,128)(2,1)S(1)} %bitcast.28), custom_call_target="tpu_custom_call" | custom-call | flops 4194304 | bytes 2097152 | tf_op jit(solution)/shard_map/extract/pallas_call | solution.py:38
  27.3 7.1 %collective-permute-start = (bf16[512,512]{1,0:T(8,128)(2,1)S(1)}, bf16[512,512]{1,0:T(8,128)(2,1)S(1)}, u32[]{:S(2)}, u32[]{:S(2)}) collective-permute-start(bf16[512,512]{1,0:T(8,128)(2,1)S(1)} %get-tuple-element.28), channel_id=1, source_target_pairs={{0,4},{1,5},{8,12},{9,13},{16,20},{17,21},{24,28},{25,29}} | collective-permute-start | bytes 1572872 | tf_op jit(solution)/shard_map/ppermute | solution.py:244
  34.4 3.8 %extract.15 = (bf16[512,512]{1,0:T(8,128)(2,1)}, f32[1,512]{1,0:T(1,128)S(1)}) custom-call(bf16[65536,128]{1,0:T(8,128)(2,1)} %bitcast.37, bf16[16,128]{1,0:T(8,128)(2,1)S(1)} %bitcast.29), custom_call_target="tpu_custom_call" | custom-call | flops 4194304 | bytes 2097152 | tf_op jit(solution)/shard_map/extract/pallas_call | solution.py:38
  38.2 3.3 %extract.10 = (bf16[512,512]{1,0:T(8,128)(2,1)S(1)}, f32[1,512]{1,0:T(1,128)S(1)}) custom-call(bf16[65536,128]{1,0:T(8,128)(2,1)} %bitcast.38, bf16[16,128]{1,0:T(8,128)(2,1)S(1)} %bitcast.30), custom_call_target="tpu_custom_call" | custom-call | flops 4194304 | bytes 2097152 | tf_op jit(solution)/shard_map/extract/pallas_call | solution.py:38
  42.3 3.3 %extract.14 = (bf16[512,512]{1,0:T(8,128)(2,1)S(1)}, f32[1,512]{1,0:T(1,128)S(1)}) custom-call(bf16[65536,128]{1,0:T(8,128)(2,1)} %bitcast.39, bf16[16,128]{1,0:T(8,128)(2,1)S(1)} %bitcast.31), custom_call_target="tpu_custom_call" | custom-call | flops 4194304 | bytes 2097152 | tf_op jit(solution)/shard_map/extract/pallas_call | solution.py:38
  46.3 3.3 %extract.9 = (bf16[512,512]{1,0:T(8,128)(2,1)S(1)}, f32[1,512]{1,0:T(1,128)S(1)}) custom-call(bf16[65536,128]{1,0:T(8,128)(2,1)} %bitcast.40, bf16[16,128]{1,0:T(8,128)(2,1)S(1)} %bitcast.32), custom_call_target="tpu_custom_call" | custom-call | flops 4194304 | bytes 2097152 | tf_op jit(solution)/shard_map/extract/pallas_call | solution.py:38
  50.6 1.6 collective-permute-start.18
  52.1 3.3 %extract.13 = (bf16[512,512]{1,0:T(8,128)(2,1)S(1)}, f32[1,512]{1,0:T(1,128)S(1)}) custom-call(bf16[65536,128]{1,0:T(8,128)(2,1)} %bitcast.41, bf16[16,128]{1,0:T(8,128)(2,1)S(1)} %bitcast.33), custom_call_target="tpu_custom_call" | custom-call | flops 4194304 | bytes 2097152 | tf_op jit(solution)/shard_map/extract/pallas_call | solution.py:38
  56.2 3.3 %extract.8 = (bf16[512,512]{1,0:T(8,128)(2,1)S(1)}, f32[1,512]{1,0:T(1,128)S(1)}) custom-call(bf16[65536,128]{1,0:T(8,128)(2,1)} %bitcast.42, bf16[16,128]{1,0:T(8,128)(2,1)S(1)} %bitcast.34), custom_call_target="tpu_custom_call" | custom-call | flops 4194304 | bytes 2097152 | tf_op jit(solution)/shard_map/extract/pallas_call | solution.py:38
  61.0 3.2 %collective-permute-done.36 = f32[8,512]{1,0:T(8,128)S(1)} collective-permute-done((f32[8,512]{1,0:T(8,128)S(1)}, f32[8,512]{1,0:T(8,128)S(1)}, u32[]{:S(2)}, u32[]{:S(2)}) %collective-permute-start.36) | collective-permute-done | bytes 16416 | tf_op jit(solution)/shard_map/ppermute | solution.py:226
  64.2 3.6 %slice.15 = bf16[512,4,4,128]{3,2,1,0:T(4,128)(2,1)} slice(bf16[4096,4,4,128]{3,2,1,0:T(4,128)(2,1)} %bitcast.43), slice={[0:512], [0:4], [0:4], [0:128]} | slice | bytes 4194304 | tf_op jit(solution)/shard_map/slice | solution.py:228
  67.9 4.7 %collective-permute-start.13 = (bf16[8192,128]{1,0:T(8,128)(2,1)}, bf16[8192,128]{1,0:T(8,128)(2,1)}, u32[]{:S(2)}, u32[]{:S(2)}) collective-permute-start(bf16[8192,128]{1,0:T(8,128)(2,1)} %bitcast.12), channel_id=1, source_target_pairs={{0,16},{8,24},{1,17},{9,25},{2,18},{10,26},{3,19},{11,27},{4,20},{... | collective-permute-start | bytes 6291464 | tf_op jit(solution)/shard_map/ppermute | solution.py:221
  77.2 8.8 %collective-permute-start.21 = (bf16[512,512]{1,0:T(8,128)(2,1)}, bf16[512,512]{1,0:T(8,128)(2,1)}, u32[]{:S(2)}, u32[]{:S(2)}) collective-permute-start(bf16[512,512]{1,0:T(8,128)(2,1)} %get-tuple-element.36), channel_id=1, source_target_pairs={{0,4},{1,5},{8,12},{9,13},{16,20},{17,21},{24,28},{25,29}} | collective-permute-start | bytes 1572872 | tf_op jit(solution)/shard_map/ppermute | solution.py:244
  91.0 23.2 %collective-permute-start.40 = (f32[4,512]{1,0:T(4,128)S(1)}, f32[4,512]{1,0:T(4,128)S(1)}, u32[]{:S(2)}, u32[]{:S(2)}) collective-permute-start(f32[4,512]{1,0:T(4,128)S(1)} %solve.5), channel_id=1, source_target_pairs={{0,8},{8,16},{16,24},{1,9},{9,17},{17,25},{2,10},{10,18},{18,26},{... | collective-permute-start | bytes 24584 | tf_op jit(solution)/shard_map/ppermute | solution.py:296
  116.0 4.4 %collective-permute-start.41 = (f32[4,512]{1,0:T(4,128)S(1)}, f32[4,512]{1,0:T(4,128)S(1)}, u32[]{:S(2)}, u32[]{:S(2)}) collective-permute-start(f32[4,512]{1,0:T(4,128)S(1)} %solve.6), channel_id=1, source_target_pairs={{0,8},{8,16},{16,24},{1,9},{9,17},{17,25},{2,10},{10,18},{18,26},{... | collective-permute-start | bytes 24584 | tf_op jit(solution)/shard_map/ppermute | solution.py:296
  120.4 2.0 select_select_fusion.7.refs_1_
  122.4 1.8 collective-permute-start.3
  125.2 2.1 collective-permute-start.42
  127.3 1.9 broadcast_select_fusion.7
  132.6 2.8 collective-permute-done.3
  135.4 1.9 broadcast_select_fusion.11
  142.5 7.7 %collective-permute-start.24 = (bf16[512,512]{1,0:T(8,128)(2,1)}, bf16[512,512]{1,0:T(8,128)(2,1)S(1)}, u32[]{:S(2)}, u32[]{:S(2)}) collective-permute-start(bf16[512,512]{1,0:T(8,128)(2,1)} %copy-done.8), channel_id=1, source_target_pairs={{0,4},{1,5},{8,12},{9,13},{16,20},{17,21},{24,28},{25,29}} | collective-permute-start | bytes 1572872 | tf_op jit(solution)/shard_map/ppermute | solution.py:244
  151.4 9.3 %collective-permute-start.6 = (bf16[512,512]{1,0:T(8,128)(2,1)}, bf16[512,512]{1,0:T(8,128)(2,1)S(1)}, u32[]{:S(2)}, u32[]{:S(2)}) collective-permute-start(bf16[512,512]{1,0:T(8,128)(2,1)} %copy-done.7), channel_id=1, source_target_pairs={{0,4},{1,5},{8,12},{9,13},{16,20},{17,21},{24,28},{25,29}} | collective-permute-start | bytes 1572872 | tf_op jit(solution)/shard_map/ppermute | solution.py:244
  160.7 1.8 broadcast_select_fusion.refs_1_
  165.6 6.2 %collective-permute-done.45 = f32[4,512]{1,0:T(4,128)S(1)} collective-permute-done((f32[4,512]{1,0:T(4,128)S(1)}, f32[4,512]{1,0:T(4,128)S(1)}, u32[]{:S(2)}, u32[]{:S(2)}) %collective-permute-start.45) | collective-permute-done | bytes 8224 | tf_op jit(solution)/shard_map/ppermute | solution.py:226
  171.8 4.4 %collective-permute-start.46 = (f32[4,512]{1,0:T(4,128)S(1)}, f32[4,512]{1,0:T(4,128)S(1)}, u32[]{:S(2)}, u32[]{:S(2)}) collective-permute-start(f32[4,512]{1,0:T(4,128)S(1)} %add.45), channel_id=1, source_target_pairs={{0,4},{1,5},{2,6},{3,7},{4,0},{5,1},{6,2},{7,3},{8,12},{9,13},{10,... | collective-permute-start | bytes 24584 | tf_op jit(solution)/shard_map/ppermute | solution.py:226
  178.0 2.2 collective-permute-done.46
  183.0 2.5 collective-permute-start.19
  185.6 8.1 %collective-permute-start.27 = (bf16[512,512]{1,0:T(8,128)(2,1)S(1)}, bf16[512,512]{1,0:T(8,128)(2,1)S(1)}, u32[]{:S(2)}, u32[]{:S(2)}) collective-permute-start(bf16[512,512]{1,0:T(8,128)(2,1)S(1)} %copy-done.6), channel_id=1, source_target_pairs={{0,4},{1,5},{8,12},{9,13},{16,20},{17,21},{24,28},{25,29}} | collective-permute-start | bytes 1572872 | tf_op jit(solution)/shard_map/ppermute | solution.py:244
  193.9 1.8 collective-permute-start.9
  196.3 9.8 %collective-permute-done.27 = bf16[512,512]{1,0:T(8,128)(2,1)S(1)} collective-permute-done((bf16[512,512]{1,0:T(8,128)(2,1)S(1)}, bf16[512,512]{1,0:T(8,128)(2,1)S(1)}, u32[]{:S(2)}, u32[]{:S(2)}) %collective-permute-start.27) | collective-permute-done | bytes 524320 | tf_op jit(solution)/shard_map/ppermute | solution.py:244
  206.9 7.3 %collective-permute-done.9 = bf16[512,512]{1,0:T(8,128)(2,1)S(1)} collective-permute-done((bf16[512,512]{1,0:T(8,128)(2,1)S(1)}, bf16[512,512]{1,0:T(8,128)(2,1)S(1)}, u32[]{:S(2)}, u32[]{:S(2)}) %collective-permute-start.9) | collective-permute-done | bytes 524320 | tf_op jit(solution)/shard_map/ppermute | solution.py:244
  217.0 22.4 %factors.1.refs_3_ = bf16[2,512,2048]{2,1,0:T(8,128)(2,1)} custom-call(s32[2]{0:T(128)S(1)} %pad_add_fusion.refs_0_, bf16[8192,128]{1,0:T(8,128)(2,1)S(1)} %broadcast_select_fusion.refs_1_, bf16[8192,128]{1,0:T(8,128)(2,1)} %copy-done.16, bf16[512,512]{1,0:T(8,128)(2,1)S(1)} %broadcast_select_fusion.4.refs_3_, ...), custom_call_target="tpu_custom_call" | custom-call | flops 6442450944 | bytes 12582912 | tf_op jit(solution)/shard_map/factors/pallas_call | solution.py:100
  243.7 2.2 copy-done
  245.9 5.8 %update.8.refs_4_ = bf16[65536,128]{1,0:T(8,128)(2,1)} custom-call(bf16[65536,128]{1,0:T(8,128)(2,1)} %bitcast.44, bf16[512,512]{1,0:T(8,128)(2,1)S(1)} %select_select_fusion.3.refs_1_, bf16[512,512]{1,0:T(8,128)(2,1)S(1)} %collective-permute-done.18.refs_2_, bf16[2,512,2048]{2,1,0:T(8,128)(2,1)S(1)} %copy-done), custom_call_target="tpu_custom_call" | custom-call | flops 2147483648 | bytes 9437184 | tf_op jit(solution)/shard_map/update/pallas_call | solution.py:144
  252.2 5.8 %update.9.refs_4_ = bf16[65536,128]{1,0:T(8,128)(2,1)} custom-call(bf16[65536,128]{1,0:T(8,128)(2,1)} %bitcast.45, bf16[512,512]{1,0:T(8,128)(2,1)S(1)} %copy-done.2, bf16[512,512]{1,0:T(8,128)(2,1)S(1)} %collective-permute-done.35.refs_2_, bf16[2,512,2048]{2,1,0:T(8,128)(2,1)S(1)} %copy-done, ...), custom_call_target="tpu_custom_call", output_to_operand_aliasing={{}: (4, {})} | custom-call | flops 2147483648 | bytes 9437184 | tf_op jit(solution)/shard_map/update/pallas_call | solution.py:144
  259.5 5.8 %update.10.refs_4_ = bf16[65536,128]{1,0:T(8,128)(2,1)} custom-call(bf16[65536,128]{1,0:T(8,128)(2,1)} %bitcast.46, bf16[512,512]{1,0:T(8,128)(2,1)S(1)} %select_select_fusion.2.refs_1_, bf16[512,512]{1,0:T(8,128)(2,1)S(1)} %collective-permute-done.34.refs_2_, bf16[2,512,2048]{2,1,0:T(8,128)(2,1)S(1)} %copy-done, ...), custom_call_target="tpu_custom_call", output_to_operand_aliasing={{}: (4, {})} | custom-call | flops 2147483648 | bytes 9437184 | tf_op jit(solution)/shard_map/update/pallas_call | solution.py:144
  265.5 5.8 %update.11.refs_4_ = bf16[65536,128]{1,0:T(8,128)(2,1)} custom-call(bf16[65536,128]{1,0:T(8,128)(2,1)} %bitcast.47, bf16[512,512]{1,0:T(8,128)(2,1)S(1)} %select_select_fusion.6.refs_1_, bf16[512,512]{1,0:T(8,128)(2,1)S(1)} %collective-permute-done.33.refs_2_, bf16[2,512,2048]{2,1,0:T(8,128)(2,1)S(1)} %copy-done, ...), custom_call_target="tpu_custom_call", output_to_operand_aliasing={{}: (4, {})} | custom-call | flops 2147483648 | bytes 9437184 | tf_op jit(solution)/shard_map/update/pallas_call | solution.py:144
  271.2 5.5 %collective-permute-done.32.refs_2_ = bf16[512,512]{1,0:T(8,128)(2,1)S(1)} collective-permute-done((bf16[512,512]{1,0:T(8,128)(2,1)S(1)}, bf16[512,512]{1,0:T(8,128)(2,1)S(1)}, u32[]{:S(2)}, u32[]{:S(2)}) %collective-permute-start.32) | collective-permute-done | bytes 524320 | tf_op jit(solution)/shard_map/ppermute | solution.py:226
  276.7 5.8 %update.12.refs_4_ = bf16[65536,128]{1,0:T(8,128)(2,1)} custom-call(bf16[65536,128]{1,0:T(8,128)(2,1)} %bitcast.48, bf16[512,512]{1,0:T(8,128)(2,1)S(1)} %select_select_fusion.1.refs_1_, bf16[512,512]{1,0:T(8,128)(2,1)S(1)} %collective-permute-done.32.refs_2_, bf16[2,512,2048]{2,1,0:T(8,128)(2,1)S(1)} %copy-done, ...), custom_call_target="tpu_custom_call", output_to_operand_aliasing={{}: (4, {})} | custom-call | flops 2147483648 | bytes 9437184 | tf_op jit(solution)/shard_map/update/pallas_call | solution.py:144
  282.5 5.5 %collective-permute-done.31.refs_2_ = bf16[512,512]{1,0:T(8,128)(2,1)S(1)} collective-permute-done((bf16[512,512]{1,0:T(8,128)(2,1)S(1)}, bf16[512,512]{1,0:T(8,128)(2,1)S(1)}, u32[]{:S(2)}, u32[]{:S(2)}) %collective-permute-start.31) | collective-permute-done | bytes 524320 | tf_op jit(solution)/shard_map/ppermute | solution.py:226
  287.9 5.8 %update.13.refs_4_ = bf16[65536,128]{1,0:T(8,128)(2,1)} custom-call(bf16[65536,128]{1,0:T(8,128)(2,1)} %bitcast.49, bf16[512,512]{1,0:T(8,128)(2,1)S(1)} %select_select_fusion.5.refs_1_, bf16[512,512]{1,0:T(8,128)(2,1)S(1)} %collective-permute-done.31.refs_2_, bf16[2,512,2048]{2,1,0:T(8,128)(2,1)S(1)} %copy-done, ...), custom_call_target="tpu_custom_call", output_to_operand_aliasing={{}: (4, {})} | custom-call | flops 2147483648 | bytes 9437184 | tf_op jit(solution)/shard_map/update/pallas_call | solution.py:144
  293.7 5.5 %collective-permute-done.30.refs_2_ = bf16[512,512]{1,0:T(8,128)(2,1)S(1)} collective-permute-done((bf16[512,512]{1,0:T(8,128)(2,1)S(1)}, bf16[512,512]{1,0:T(8,128)(2,1)S(1)}, u32[]{:S(2)}, u32[]{:S(2)}) %collective-permute-start.30) | collective-permute-done | bytes 524320 | tf_op jit(solution)/shard_map/ppermute | solution.py:226
  299.2 6.0 %update.14.refs_4_ = bf16[65536,128]{1,0:T(8,128)(2,1)} custom-call(bf16[65536,128]{1,0:T(8,128)(2,1)} %bitcast.50, bf16[512,512]{1,0:T(8,128)(2,1)S(1)} %select_select_fusion.refs_1_, bf16[512,512]{1,0:T(8,128)(2,1)S(1)} %collective-permute-done.30.refs_2_, bf16[2,512,2048]{2,1,0:T(8,128)(2,1)S(1)} %copy-done, ...), custom_call_target="tpu_custom_call", output_to_operand_aliasing={{}: (4, {})} | custom-call | flops 2147483648 | bytes 9437184 | tf_op jit(solution)/shard_map/update/pallas_call | solution.py:144
  306.3 5.8 %update.15 = bf16[65536,128]{1,0:T(8,128)(2,1)} custom-call(bf16[65536,128]{1,0:T(8,128)(2,1)} %bitcast.51, bf16[512,512]{1,0:T(8,128)(2,1)S(1)} %select_select_fusion.4.refs_1_, bf16[512,512]{1,0:T(8,128)(2,1)S(1)} %collective-permute-done.12.refs_2_, bf16[2,512,2048]{2,1,0:T(8,128)(2,1)S(1)} %copy-done, ...), custom_call_target="tpu_custom_call", output_to_operand_aliasing={{}: (4, {})} | custom-call | flops 2147483648 | bytes 9437184 | tf_op jit(solution)/shard_map/update/pallas_call | solution.py:144
  (135 shorter events, 49.4 us)
Async XLA Ops:
  4.6 17.1 %collective-permute-start.15 = (bf16[512,512]{1,0:T(8,128)(2,1)S(1)}, bf16[512,512]{1,0:T(8,128)(2,1)S(1)}, u32[]{:S(2)}, u32[]{:S(2)}) collective-permute-start(bf16[512,512]{1,0:T(8,128)(2,1)S(1)} %get-tuple-element.32.rest_2_), channel_id=1, source_target_pairs={{0,4},{1,5},{8,12},{9,13},{16,20},{17,21},{24,28},{25,29}} | collective-permute-start | bytes 1572872 | tf_op jit(solution)/shard_map/ppermute | solution.py:244
  21.8 28.7 %collective-permute-start.16 = (bf16[512,512]{1,0:T(8,128)(2,1)S(1)}, bf16[512,512]{1,0:T(8,128)(2,1)S(1)}, u32[]{:S(2)}, u32[]{:S(2)}) collective-permute-start(bf16[512,512]{1,0:T(8,128)(2,1)S(1)} %broadcast_select_fusion.8), channel_id=1, source_target_pairs={{4,6},{5,7},{12,14},{13,15},{20,22},{21,23},{28,30},{29,31}} | collective-permute-start | bytes 1572872 | tf_op jit(solution)/shard_map/ppermute | solution.py:244
  22.5 28.0 %collective-permute-start.17 = (bf16[512,512]{1,0:T(8,128)(2,1)S(1)}, bf16[512,512]{1,0:T(8,128)(2,1)}, u32[]{:S(2)}, u32[]{:S(2)}) collective-permute-start(bf16[512,512]{1,0:T(8,128)(2,1)S(1)} %broadcast_select_fusion.8), channel_id=1, source_target_pairs={{4,2},{5,3},{12,10},{13,11},{20,18},{21,19},{28,26},{29,27}} | collective-permute-start | bytes 1572872 | tf_op jit(solution)/shard_map/ppermute | solution.py:244
  27.3 45.3 %collective-permute-start = (bf16[512,512]{1,0:T(8,128)(2,1)S(1)}, bf16[512,512]{1,0:T(8,128)(2,1)S(1)}, u32[]{:S(2)}, u32[]{:S(2)}) collective-permute-start(bf16[512,512]{1,0:T(8,128)(2,1)S(1)} %get-tuple-element.28), channel_id=1, source_target_pairs={{0,4},{1,5},{8,12},{9,13},{16,20},{17,21},{24,28},{25,29}} | collective-permute-start | bytes 1572872 | tf_op jit(solution)/shard_map/ppermute | solution.py:244
  50.6 35.5 %collective-permute-start.18 = (bf16[512,512]{1,0:T(8,128)(2,1)S(1)}, bf16[512,512]{1,0:T(8,128)(2,1)S(1)}, u32[]{:S(2)}, u32[]{:S(2)}) collective-permute-start(bf16[512,512]{1,0:T(8,128)(2,1)S(1)} %select_select_fusion.3.refs_1_), channel_id=1, source_target_pairs={{0,1},{1,0},{2,3},{3,2},{4,5},{5,4},{6,7},{7,6},{8,9},{9,8},{10,11... | collective-permute-start | bytes 1572872 | tf_op jit(solution)/shard_map/ppermute | solution.py:226
  60.4 3.8 %collective-permute-start.36 = (f32[8,512]{1,0:T(8,128)S(1)}, f32[8,512]{1,0:T(8,128)S(1)}, u32[]{:S(2)}, u32[]{:S(2)}) collective-permute-start(f32[8,512]{1,0:T(8,128)S(1)} %concatenate.3), channel_id=1, source_target_pairs={{0,1},{1,0},{2,3},{3,2},{4,5},{5,4},{6,7},{7,6},{8,9},{9,8},{10,11... | collective-permute-start | bytes 49160 | tf_op jit(solution)/shard_map/ppermute | solution.py:226
  64.2 8.4 %collective-permute-start.37 = (f32[8,512]{1,0:T(8,128)S(1)}, f32[8,512]{1,0:T(8,128)S(1)}, u32[]{:S(2)}, u32[]{:S(2)}) collective-permute-start(f32[8,512]{1,0:T(8,128)S(1)} %add.39), channel_id=1, source_target_pairs={{0,2},{1,3},{2,0},{3,1},{4,6},{5,7},{6,4},{7,5},{8,10},{9,11},{10,... | collective-permute-start | bytes 49160 | tf_op jit(solution)/shard_map/ppermute | solution.py:226
  67.9 92.9 %collective-permute-start.13 = (bf16[8192,128]{1,0:T(8,128)(2,1)}, bf16[8192,128]{1,0:T(8,128)(2,1)}, u32[]{:S(2)}, u32[]{:S(2)}) collective-permute-start(bf16[8192,128]{1,0:T(8,128)(2,1)} %bitcast.12), channel_id=1, source_target_pairs={{0,16},{8,24},{1,17},{9,25},{2,18},{10,26},{3,19},{11,27},{4,20},{... | collective-permute-start | bytes 6291464 | tf_op jit(solution)/shard_map/ppermute | solution.py:221
  72.6 4.6 %collective-permute-start.38 = (f32[8,512]{1,0:T(8,128)S(1)}, f32[8,512]{1,0:T(8,128)S(1)}, u32[]{:S(2)}, u32[]{:S(2)}) collective-permute-start(f32[8,512]{1,0:T(8,128)S(1)} %add.40), channel_id=1, source_target_pairs={{0,4},{1,5},{2,6},{3,7},{4,0},{5,1},{6,2},{7,3},{8,12},{9,13},{10,... | collective-permute-start | bytes 49160 | tf_op jit(solution)/shard_map/ppermute | solution.py:226
  73.5 46.9 %collective-permute-start.1 = (bf16[512,512]{1,0:T(8,128)(2,1)}, bf16[512,512]{1,0:T(8,128)(2,1)}, u32[]{:S(2)}, u32[]{:S(2)}) collective-permute-start(bf16[512,512]{1,0:T(8,128)(2,1)} %broadcast_select_fusion.12), channel_id=1, source_target_pairs={{4,6},{5,7},{12,14},{13,15},{20,22},{21,23},{28,30},{29,31}} | collective-permute-start | bytes 1572872 | tf_op jit(solution)/shard_map/ppermute | solution.py:244
  75.0 45.4 %collective-permute-start.2 = (bf16[512,512]{1,0:T(8,128)(2,1)}, bf16[512,512]{1,0:T(8,128)(2,1)}, u32[]{:S(2)}, u32[]{:S(2)}) collective-permute-start(bf16[512,512]{1,0:T(8,128)(2,1)} %broadcast_select_fusion.12), channel_id=1, source_target_pairs={{4,2},{5,3},{12,10},{13,11},{20,18},{21,19},{28,26},{29,27}} | collective-permute-start | bytes 1572872 | tf_op jit(solution)/shard_map/ppermute | solution.py:244
  77.2 50.1 %collective-permute-start.21 = (bf16[512,512]{1,0:T(8,128)(2,1)}, bf16[512,512]{1,0:T(8,128)(2,1)}, u32[]{:S(2)}, u32[]{:S(2)}) collective-permute-start(bf16[512,512]{1,0:T(8,128)(2,1)} %get-tuple-element.36), channel_id=1, source_target_pairs={{0,4},{1,5},{8,12},{9,13},{16,20},{17,21},{24,28},{25,29}} | collective-permute-start | bytes 1572872 | tf_op jit(solution)/shard_map/ppermute | solution.py:244
  87.9 2.1 collective-permute-start.39
  91.0 24.0 %collective-permute-start.40 = (f32[4,512]{1,0:T(4,128)S(1)}, f32[4,512]{1,0:T(4,128)S(1)}, u32[]{:S(2)}, u32[]{:S(2)}) collective-permute-start(f32[4,512]{1,0:T(4,128)S(1)} %solve.5), channel_id=1, source_target_pairs={{0,8},{8,16},{16,24},{1,9},{9,17},{17,25},{2,10},{10,18},{18,26},{... | collective-permute-start | bytes 24584 | tf_op jit(solution)/shard_map/ppermute | solution.py:296
  116.0 8.2 %collective-permute-start.41 = (f32[4,512]{1,0:T(4,128)S(1)}, f32[4,512]{1,0:T(4,128)S(1)}, u32[]{:S(2)}, u32[]{:S(2)}) collective-permute-start(f32[4,512]{1,0:T(4,128)S(1)} %solve.6), channel_id=1, source_target_pairs={{0,8},{8,16},{16,24},{1,9},{9,17},{17,25},{2,10},{10,18},{18,26},{... | collective-permute-start | bytes 24584 | tf_op jit(solution)/shard_map/ppermute | solution.py:296
  122.4 13.1 %collective-permute-start.3 = (bf16[512,512]{1,0:T(8,128)(2,1)}, bf16[512,512]{1,0:T(8,128)(2,1)S(1)}, u32[]{:S(2)}, u32[]{:S(2)}) collective-permute-start(bf16[512,512]{1,0:T(8,128)(2,1)} %copy-done.9), channel_id=1, source_target_pairs={{0,4},{1,5},{8,12},{9,13},{16,20},{17,21},{24,28},{25,29}} | collective-permute-start | bytes 1572872 | tf_op jit(solution)/shard_map/ppermute | solution.py:244
  125.2 91.8 %copy-start.12 = (bf16[2,512,512]{2,1,0:T(8,128)(2,1)S(1)}, bf16[2,512,512]{2,1,0:T(8,128)(2,1)}, u32[]{:S(2)}) copy-start(bf16[2,512,512]{2,1,0:T(8,128)(2,1)} %refs_5_.1) | copy-start | bytes 3145732
  125.2 6.9 %collective-permute-start.42 = (f32[4,512]{1,0:T(4,128)S(1)}, f32[4,512]{1,0:T(4,128)S(1)}, u32[]{:S(2)}, u32[]{:S(2)}) collective-permute-start(f32[4,512]{1,0:T(4,128)S(1)} %broadcast_select_fusion.13), channel_id=1, source_target_pairs={{0,8},{8,0},{16,24},{24,16},{1,9},{9,1},{17,25},{25,17},{2,10},{10... | collective-permute-start | bytes 24584 | tf_op jit(solution)/shard_map/ppermute | solution.py:226
  129.2 11.1 %collective-permute-start.22 = (bf16[512,512]{1,0:T(8,128)(2,1)}, bf16[512,512]{1,0:T(8,128)(2,1)}, u32[]{:S(2)}, u32[]{:S(2)}) collective-permute-start(bf16[512,512]{1,0:T(8,128)(2,1)} %broadcast_select_fusion.7), channel_id=1, source_target_pairs={{4,6},{5,7},{12,14},{13,15},{20,22},{21,23},{28,30},{29,31}} | collective-permute-start | bytes 1572872 | tf_op jit(solution)/shard_map/ppermute | solution.py:244
  130.7 10.7 %collective-permute-start.23 = (bf16[512,512]{1,0:T(8,128)(2,1)}, bf16[512,512]{1,0:T(8,128)(2,1)}, u32[]{:S(2)}, u32[]{:S(2)}) collective-permute-start(bf16[512,512]{1,0:T(8,128)(2,1)} %broadcast_select_fusion.7), channel_id=1, source_target_pairs={{4,2},{5,3},{12,10},{13,11},{20,18},{21,19},{28,26},{29,27}} | collective-permute-start | bytes 1572872 | tf_op jit(solution)/shard_map/ppermute | solution.py:244
  132.2 6.6 %collective-permute-start.43 = (f32[4,512]{1,0:T(4,128)S(1)}, f32[4,512]{1,0:T(4,128)S(1)}, u32[]{:S(2)}, u32[]{:S(2)}) collective-permute-start(f32[4,512]{1,0:T(4,128)S(1)} %fusion), channel_id=1, source_target_pairs={{0,16},{8,24},{16,0},{24,8},{1,17},{9,25},{17,1},{25,9},{2,18},{10... | collective-permute-start | bytes 24584 | tf_op jit(solution)/shard_map/ppermute | solution.py:226
  137.3 12.9 %collective-permute-start.4 = (bf16[512,512]{1,0:T(8,128)(2,1)}, bf16[512,512]{1,0:T(8,128)(2,1)}, u32[]{:S(2)}, u32[]{:S(2)}) collective-permute-start(bf16[512,512]{1,0:T(8,128)(2,1)} %broadcast_select_fusion.11), channel_id=1, source_target_pairs={{4,6},{5,7},{12,14},{13,15},{20,22},{21,23},{28,30},{29,31}} | collective-permute-start | bytes 1572872 | tf_op jit(solution)/shard_map/ppermute | solution.py:244
  138.8 11.5 %collective-permute-start.5 = (bf16[512,512]{1,0:T(8,128)(2,1)}, bf16[512,512]{1,0:T(8,128)(2,1)}, u32[]{:S(2)}, u32[]{:S(2)}) collective-permute-start(bf16[512,512]{1,0:T(8,128)(2,1)} %broadcast_select_fusion.11), channel_id=1, source_target_pairs={{4,2},{5,3},{12,10},{13,11},{20,18},{21,19},{28,26},{29,27}} | collective-permute-start | bytes 1572872 | tf_op jit(solution)/shard_map/ppermute | solution.py:244
  140.3 24.9 %collective-permute-start.44 = (f32[4,512]{1,0:T(4,128)S(1)}, f32[4,512]{1,0:T(4,128)S(1)}, u32[]{:S(2)}, u32[]{:S(2)}) collective-permute-start(f32[4,512]{1,0:T(4,128)S(1)} %add.43), channel_id=1, source_target_pairs={{0,1},{1,0},{2,3},{3,2},{4,5},{5,4},{6,7},{7,6},{8,9},{9,8},{10,11... | collective-permute-start | bytes 24584 | tf_op jit(solution)/shard_map/ppermute | solution.py:226
  142.5 20.1 %collective-permute-start.24 = (bf16[512,512]{1,0:T(8,128)(2,1)}, bf16[512,512]{1,0:T(8,128)(2,1)S(1)}, u32[]{:S(2)}, u32[]{:S(2)}) collective-permute-start(bf16[512,512]{1,0:T(8,128)(2,1)} %copy-done.8), channel_id=1, source_target_pairs={{0,4},{1,5},{8,12},{9,13},{16,20},{17,21},{24,28},{25,29}} | collective-permute-start | bytes 1572872 | tf_op jit(solution)/shard_map/ppermute | solution.py:244
  151.4 24.8 %collective-permute-start.6 = (bf16[512,512]{1,0:T(8,128)(2,1)}, bf16[512,512]{1,0:T(8,128)(2,1)S(1)}, u32[]{:S(2)}, u32[]{:S(2)}) collective-permute-start(bf16[512,512]{1,0:T(8,128)(2,1)} %copy-done.7), channel_id=1, source_target_pairs={{0,4},{1,5},{8,12},{9,13},{16,20},{17,21},{24,28},{25,29}} | collective-permute-start | bytes 1572872 | tf_op jit(solution)/shard_map/ppermute | solution.py:244
  162.5 53.1 %collective-permute-start.14 = (bf16[8192,128]{1,0:T(8,128)(2,1)S(1)}, bf16[8192,128]{1,0:T(8,128)(2,1)S(1)}, u32[]{:S(2)}, u32[]{:S(2)}) collective-permute-start(bf16[8192,128]{1,0:T(8,128)(2,1)S(1)} %broadcast_select_fusion.refs_1_), channel_id=1, source_target_pairs={{0,8},{8,0},{16,24},{24,16},{1,9},{9,1},{17,25},{25,17},{2,10},{10... | collective-permute-start | bytes 6291464 | tf_op jit(solution)/shard_map/ppermute | solution.py:226
  163.7 18.5 %collective-permute-start.25 = (bf16[512,512]{1,0:T(8,128)(2,1)S(1)}, bf16[512,512]{1,0:T(8,128)(2,1)S(1)}, u32[]{:S(2)}, u32[]{:S(2)}) collective-permute-start(bf16[512,512]{1,0:T(8,128)(2,1)S(1)} %broadcast_select_fusion.6), channel_id=1, source_target_pairs={{4,6},{5,7},{12,14},{13,15},{20,22},{21,23},{28,30},{29,31}} | collective-permute-start | bytes 1572872 | tf_op jit(solution)/shard_map/ppermute | solution.py:244
  164.4 18.5 %collective-permute-start.26 = (bf16[512,512]{1,0:T(8,128)(2,1)S(1)}, bf16[512,512]{1,0:T(8,128)(2,1)S(1)}, u32[]{:S(2)}, u32[]{:S(2)}) collective-permute-start(bf16[512,512]{1,0:T(8,128)(2,1)S(1)} %broadcast_select_fusion.6), channel_id=1, source_target_pairs={{4,2},{5,3},{12,10},{13,11},{20,18},{21,19},{28,26},{29,27}} | collective-permute-start | bytes 1572872 | tf_op jit(solution)/shard_map/ppermute | solution.py:244
  165.2 6.6 %collective-permute-start.45 = (f32[4,512]{1,0:T(4,128)S(1)}, f32[4,512]{1,0:T(4,128)S(1)}, u32[]{:S(2)}, u32[]{:S(2)}) collective-permute-start(f32[4,512]{1,0:T(4,128)S(1)} %add.44), channel_id=1, source_target_pairs={{0,2},{1,3},{2,0},{3,1},{4,6},{5,7},{6,4},{7,5},{8,10},{9,11},{10,... | collective-permute-start | bytes 24584 | tf_op jit(solution)/shard_map/ppermute | solution.py:226
  171.8 8.4 %collective-permute-start.46 = (f32[4,512]{1,0:T(4,128)S(1)}, f32[4,512]{1,0:T(4,128)S(1)}, u32[]{:S(2)}, u32[]{:S(2)}) collective-permute-start(f32[4,512]{1,0:T(4,128)S(1)} %add.45), channel_id=1, source_target_pairs={{0,4},{1,5},{2,6},{3,7},{4,0},{5,1},{6,2},{7,3},{8,12},{9,13},{10,... | collective-permute-start | bytes 24584 | tf_op jit(solution)/shard_map/ppermute | solution.py:226
  177.3 8.3 %collective-permute-start.7 = (bf16[512,512]{1,0:T(8,128)(2,1)S(1)}, bf16[512,512]{1,0:T(8,128)(2,1)S(1)}, u32[]{:S(2)}, u32[]{:S(2)}) collective-permute-start(bf16[512,512]{1,0:T(8,128)(2,1)S(1)} %broadcast_select_fusion.10), channel_id=1, source_target_pairs={{4,6},{5,7},{12,14},{13,15},{20,22},{21,23},{28,30},{29,31}} | collective-permute-start | bytes 1572872 | tf_op jit(solution)/shard_map/ppermute | solution.py:244
  180.2 13.6 %collective-permute-start.8 = (bf16[512,512]{1,0:T(8,128)(2,1)S(1)}, bf16[512,512]{1,0:T(8,128)(2,1)S(1)}, u32[]{:S(2)}, u32[]{:S(2)}) collective-permute-start(bf16[512,512]{1,0:T(8,128)(2,1)S(1)} %broadcast_select_fusion.10), channel_id=1, source_target_pairs={{4,2},{5,3},{12,10},{13,11},{20,18},{21,19},{28,26},{29,27}} | collective-permute-start | bytes 1572872 | tf_op jit(solution)/shard_map/ppermute | solution.py:244
  182.2 69.5 %collective-permute-start.35 = (bf16[512,512]{1,0:T(8,128)(2,1)S(1)}, bf16[512,512]{1,0:T(8,128)(2,1)S(1)}, u32[]{:S(2)}, u32[]{:S(2)}) collective-permute-start(bf16[512,512]{1,0:T(8,128)(2,1)S(1)} %copy-done.2), channel_id=1, source_target_pairs={{0,1},{1,0},{2,3},{3,2},{4,5},{5,4},{6,7},{7,6},{8,9},{9,8},{10,11... | collective-permute-start | bytes 1572872 | tf_op jit(solution)/shard_map/ppermute | solution.py:226
  183.0 13.2 %collective-permute-start.19 = (bf16[512,512]{1,0:T(8,128)(2,1)}, bf16[512,512]{1,0:T(8,128)(2,1)S(1)}, u32[]{:S(2)}, u32[]{:S(2)}) collective-permute-start(bf16[512,512]{1,0:T(8,128)(2,1)} %get-tuple-element.52), channel_id=1, source_target_pairs={{0,16},{8,24},{1,17},{9,25},{2,18},{10,26},{3,19},{11,27},{4,20},{... | collective-permute-start | bytes 1572872 | tf_op jit(solution)/shard_map/ppermute | solution.py:221
  185.6 20.5 %collective-permute-start.27 = (bf16[512,512]{1,0:T(8,128)(2,1)S(1)}, bf16[512,512]{1,0:T(8,128)(2,1)S(1)}, u32[]{:S(2)}, u32[]{:S(2)}) collective-permute-start(bf16[512,512]{1,0:T(8,128)(2,1)S(1)} %copy-done.6), channel_id=1, source_target_pairs={{0,4},{1,5},{8,12},{9,13},{16,20},{17,21},{24,28},{25,29}} | collective-permute-start | bytes 1572872 | tf_op jit(solution)/shard_map/ppermute | solution.py:244
  193.9 20.3 %collective-permute-start.9 = (bf16[512,512]{1,0:T(8,128)(2,1)S(1)}, bf16[512,512]{1,0:T(8,128)(2,1)S(1)}, u32[]{:S(2)}, u32[]{:S(2)}) collective-permute-start(bf16[512,512]{1,0:T(8,128)(2,1)S(1)} %copy-done.4), channel_id=1, source_target_pairs={{0,4},{1,5},{8,12},{9,13},{16,20},{17,21},{24,28},{25,29}} | collective-permute-start | bytes 1572872 | tf_op jit(solution)/shard_map/ppermute | solution.py:244
  196.2 18.7 %collective-permute-start.20 = (bf16[512,512]{1,0:T(8,128)(2,1)S(1)}, bf16[512,512]{1,0:T(8,128)(2,1)S(1)}, u32[]{:S(2)}, u32[]{:S(2)}) collective-permute-start(bf16[512,512]{1,0:T(8,128)(2,1)S(1)} %broadcast_select_fusion.4.refs_3_), channel_id=1, source_target_pairs={{0,8},{8,0},{16,24},{24,16},{1,9},{9,1},{17,25},{25,17},{2,10},{10... | collective-permute-start | bytes 1572872 | tf_op jit(solution)/shard_map/ppermute | solution.py:226
  206.2 33.2 %collective-permute-start.28 = (bf16[512,512]{1,0:T(8,128)(2,1)S(1)}, bf16[512,512]{1,0:T(8,128)(2,1)S(1)}, u32[]{:S(2)}, u32[]{:S(2)}) collective-permute-start(bf16[512,512]{1,0:T(8,128)(2,1)S(1)} %broadcast_select_fusion.5), channel_id=1, source_target_pairs={{4,6},{5,7},{12,14},{13,15},{20,22},{21,23},{28,30},{29,31}} | collective-permute-start | bytes 1572872 | tf_op jit(solution)/shard_map/ppermute | solution.py:244
  214.2 25.8 %collective-permute-start.29 = (bf16[512,512]{1,0:T(8,128)(2,1)S(1)}, bf16[512,512]{1,0:T(8,128)(2,1)S(1)}, u32[]{:S(2)}, u32[]{:S(2)}) collective-permute-start(bf16[512,512]{1,0:T(8,128)(2,1)S(1)} %broadcast_select_fusion.5), channel_id=1, source_target_pairs={{4,2},{5,3},{12,10},{13,11},{20,18},{21,19},{28,26},{29,27}} | collective-permute-start | bytes 1572872 | tf_op jit(solution)/shard_map/ppermute | solution.py:244
  214.9 26.5 %collective-permute-start.10 = (bf16[512,512]{1,0:T(8,128)(2,1)S(1)}, bf16[512,512]{1,0:T(8,128)(2,1)S(1)}, u32[]{:S(2)}, u32[]{:S(2)}) collective-permute-start(bf16[512,512]{1,0:T(8,128)(2,1)S(1)} %broadcast_select_fusion.9), channel_id=1, source_target_pairs={{4,6},{5,7},{12,14},{13,15},{20,22},{21,23},{28,30},{29,31}} | collective-permute-start | bytes 1572872 | tf_op jit(solution)/shard_map/ppermute | solution.py:244
  215.7 26.5 %collective-permute-start.11 = (bf16[512,512]{1,0:T(8,128)(2,1)S(1)}, bf16[512,512]{1,0:T(8,128)(2,1)S(1)}, u32[]{:S(2)}, u32[]{:S(2)}) collective-permute-start(bf16[512,512]{1,0:T(8,128)(2,1)S(1)} %broadcast_select_fusion.9), channel_id=1, source_target_pairs={{4,2},{5,3},{12,10},{13,11},{20,18},{21,19},{28,26},{29,27}} | collective-permute-start | bytes 1572872 | tf_op jit(solution)/shard_map/ppermute | solution.py:244
  239.4 18.7 %collective-permute-start.34 = (bf16[512,512]{1,0:T(8,128)(2,1)S(1)}, bf16[512,512]{1,0:T(8,128)(2,1)S(1)}, u32[]{:S(2)}, u32[]{:S(2)}) collective-permute-start(bf16[512,512]{1,0:T(8,128)(2,1)S(1)} %select_select_fusion.2.refs_1_), channel_id=1, source_target_pairs={{0,1},{1,0},{2,3},{3,2},{4,5},{5,4},{6,7},{7,6},{8,9},{9,8},{10,11... | collective-permute-start | bytes 1572872 | tf_op jit(solution)/shard_map/ppermute | solution.py:226
  239.9 25.5 %collective-permute-start.33 = (bf16[512,512]{1,0:T(8,128)(2,1)S(1)}, bf16[512,512]{1,0:T(8,128)(2,1)S(1)}, u32[]{:S(2)}, u32[]{:S(2)}) collective-permute-start(bf16[512,512]{1,0:T(8,128)(2,1)S(1)} %select_select_fusion.6.refs_1_), channel_id=1, source_target_pairs={{0,1},{1,0},{2,3},{3,2},{4,5},{5,4},{6,7},{7,6},{8,9},{9,8},{10,11... | collective-permute-start | bytes 1572872 | tf_op jit(solution)/shard_map/ppermute | solution.py:226
  241.5 35.2 %collective-permute-start.32 = (bf16[512,512]{1,0:T(8,128)(2,1)S(1)}, bf16[512,512]{1,0:T(8,128)(2,1)S(1)}, u32[]{:S(2)}, u32[]{:S(2)}) collective-permute-start(bf16[512,512]{1,0:T(8,128)(2,1)S(1)} %select_select_fusion.1.refs_1_), channel_id=1, source_target_pairs={{0,1},{1,0},{2,3},{3,2},{4,5},{5,4},{6,7},{7,6},{8,9},{9,8},{10,11... | collective-permute-start | bytes 1572872 | tf_op jit(solution)/shard_map/ppermute | solution.py:226
  242.1 45.8 %collective-permute-start.31 = (bf16[512,512]{1,0:T(8,128)(2,1)S(1)}, bf16[512,512]{1,0:T(8,128)(2,1)S(1)}, u32[]{:S(2)}, u32[]{:S(2)}) collective-permute-start(bf16[512,512]{1,0:T(8,128)(2,1)S(1)} %select_select_fusion.5.refs_1_), channel_id=1, source_target_pairs={{0,1},{1,0},{2,3},{3,2},{4,5},{5,4},{6,7},{7,6},{8,9},{9,8},{10,11... | collective-permute-start | bytes 1572872 | tf_op jit(solution)/shard_map/ppermute | solution.py:226
  251.7 47.5 %collective-permute-start.30 = (bf16[512,512]{1,0:T(8,128)(2,1)S(1)}, bf16[512,512]{1,0:T(8,128)(2,1)S(1)}, u32[]{:S(2)}, u32[]{:S(2)}) collective-permute-start(bf16[512,512]{1,0:T(8,128)(2,1)S(1)} %select_select_fusion.refs_1_), channel_id=1, source_target_pairs={{0,1},{1,0},{2,3},{3,2},{4,5},{5,4},{6,7},{7,6},{8,9},{9,8},{10,11... | collective-permute-start | bytes 1572872 | tf_op jit(solution)/shard_map/ppermute | solution.py:226
  258.0 48.3 %collective-permute-start.12 = (bf16[512,512]{1,0:T(8,128)(2,1)S(1)}, bf16[512,512]{1,0:T(8,128)(2,1)S(1)}, u32[]{:S(2)}, u32[]{:S(2)}) collective-permute-start(bf16[512,512]{1,0:T(8,128)(2,1)S(1)} %select_select_fusion.4.refs_1_), channel_id=1, source_target_pairs={{0,1},{1,0},{2,3},{3,2},{4,5},{5,4},{6,7},{7,6},{8,9},{9,8},{10,11... | collective-permute-start | bytes 1572872 | tf_op jit(solution)/shard_map/ppermute | solution.py:226
  (16 other events, 402.4 us)
